TPU v7x, 32 devices: a whole 2x2x4 slice. The times are simulated.
32 devices in a mesh: rows: 8 (over z, y), shock: 4 (over x, core).
Axes of the slice: x: 2, y: 2, z: 4, core: 2. Of those that a mesh axis runs over, the one named last changes fastest.
Arguments:
- coefs: bfloat16 [32, 16, 128, 128], P('rows'), may hold values from -0.125 to 0.125
- lag_pattern: int32 [32, 16], replicated, may hold values from 0 to 31, as said below
- loadings: float32 [4096, 128], P('rows'), may hold values from -0.5 to 0.5
- idiosyncratic: float32 [4096], P('rows'), may hold values from 0.5 to 2
- shocked: int32 [512], P('shock'), may hold values from 0 to 4095
Outputs:
- shares: float32 [4096, 512], P('rows', 'shock')
Inputs may be any that keep to these rules, and one draw needn't show every extreme that they name: `lag_pattern`: each row holds distinct blocks. The block rows held by any one device along `rows` together read exactly 4 distinct block from the 4 blocks held by every device along `rows`.
All inputs are finite; a program needn't handle non-finite values.
Results may differ from a plain program's by a relative error of at most 0.009.
Values may be sent and summed in bfloat16 or wider, within the bound.
A program may use at most 64 MiB of HBM per device.

v0:
```python
import jax
import jax.numpy as jnp
from jax import lax
from jax.sharding import PartitionSpec as P

HORIZONS = 7


def on_device(coefs, lag_pattern, loadings, idiosyncratic, shocked):
    blk_dev = coefs.shape[0]
    lags = coefs.shape[1]
    block_size = coefs.shape[2]
    owners = lax.axis_size("rows")
    mine = lax.axis_index("rows")
    n_blocks = owners * blk_dev
    capacity = min(blk_dev, max(1, blk_dev * lags // owners))
    shock_columns = shocked.shape[0]
    local_rows = blk_dev * block_size
    row_ids = mine * local_rows + jnp.arange(local_rows, dtype=jnp.int32)
    pick_table = (shocked[:, None] == row_ids[None, :]).astype(jnp.float32)
    chosen = jnp.dot(
        pick_table, loadings, precision=lax.Precision.HIGHEST, preferred_element_type=jnp.float32
    )
    chosen_idio = jnp.dot(
        pick_table,
        idiosyncratic,
        precision=lax.Precision.HIGHEST,
        preferred_element_type=jnp.float32,
    )
    chosen, chosen_idio = lax.psum((chosen, chosen_idio), "rows")
    scale = jnp.sqrt(jnp.sum(chosen * chosen, axis=1) + chosen_idio)
    impact = jnp.dot(
        loadings, chosen.T, precision=lax.Precision.HIGHEST, preferred_element_type=jnp.float32
    )
    impact = impact + pick_table.T * idiosyncratic[:, None]
    impact = impact / scale[None, :]
    present_response = impact.astype(jnp.bfloat16).reshape(blk_dev, block_size, shock_columns)
    squared_terms = present_response.astype(jnp.float32) ** 2
    my_lags = lax.dynamic_slice_in_dim(lag_pattern, mine * blk_dev, blk_dev, 0)
    flat_lags = my_lags.reshape(-1)
    all_blocks_ids = jnp.arange(n_blocks, dtype=jnp.int32)
    read_need = jnp.any(flat_lags[:, None] == all_blocks_ids[None, :], axis=0).astype(jnp.int32)
    read_need = read_need.reshape(owners, blk_dev)
    read_before = jnp.cumsum(read_need, axis=1) - read_need
    owner_base = jnp.arange(owners, dtype=jnp.int32)[:, None] * capacity
    slot_of_block = (owner_base + read_before).reshape(-1)
    take_index = slot_of_block[flat_lags]
    reader_slots = lag_pattern.reshape(owners, blk_dev * lags)
    own_ids = mine * blk_dev + jnp.arange(blk_dev, dtype=jnp.int32)
    send_need = jnp.any(reader_slots[:, :, None] == own_ids[None, None, :], axis=1).astype(
        jnp.int32
    )
    send_before = jnp.cumsum(send_need, axis=1) - send_need
    cap_pos = jnp.arange(capacity, dtype=jnp.int32)
    routing_matrix = (
        (send_need[:, None, :] == 1) & (send_before[:, None, :] == cap_pos[None, :, None])
    ).astype(jnp.bfloat16)
    for step in range(HORIZONS - 1):
        outgoing = jnp.einsum(
            "vwq,qfn->vwfn", routing_matrix, present_response, preferred_element_type=jnp.float32
        ).astype(jnp.bfloat16)
        arriving_response = lax.all_to_all(
            outgoing, "rows", split_axis=0, concat_axis=0, tiled=True
        )
        stacked = arriving_response.reshape(owners * capacity, block_size, shock_columns)
        lagged = jnp.take(stacked, take_index, axis=0).reshape(
            blk_dev, lags, block_size, shock_columns
        )
        product = jnp.einsum("rlij,rljs->ris", coefs, lagged, preferred_element_type=jnp.float32)
        present_response = product.astype(jnp.bfloat16)
        squared_terms = squared_terms + present_response.astype(jnp.float32) ** 2
    totals = lax.psum(jnp.sum(squared_terms, axis=2), "shock")
    total_shocks = shock_columns * lax.axis_size("shock")
    shares = total_shocks * squared_terms / (totals[:, :, None] + 1e-06)
    return shares.reshape(local_rows, shock_columns)


def solution(mesh):
    placed = (P("rows", None, None, None), P(), P("rows", None), P("rows"), P("shock"))
    return jax.shard_map(
        on_device, mesh=mesh, in_specs=placed, out_specs=P("rows", "shock"), check_vma=False
    )
```

profile of v0, /device:TPU:0, one launch (start us, length us, event | category | flops | bytes accessed | tf_op | source)
XLA Modules:
  0.0 306.4 jit_solution(1372096305009810286)
XLA Ops:
  6.5 2.1 fusion.19
  9.8 0.9 convolution_bitcast_fusion.7
  10.7 23.2 %psum.22 = f32[128]{0:T(128)S(1)} all-reduce(f32[128]{0:T(128)S(1)} %convolution_bitcast_fusion.7), channel_id=1, replica_groups=mesh['rows'=8,'shock'=4] {'rows'}, use_global_device_ids=true, to_apply=%region_2.0 | all-reduce | flops 128 | bytes 1024 | tf_op jit(solution)/shard_map/psum | solution.py:30
  33.9 48.1 %all-reduce.2.cloned.1.call-done = f32[128,128]{1,0:T(8,128)} async-done(((f32[128,128]{1,0:T(8,128)}), f32[128,128]{1,0:T(8,128)}) %all-reduce.2.cloned.1.call-update) | async-done | bytes 65552 | tf_op jit(solution)/shard_map/psum | solution.py:30
  82.0 0.9 multiply_reduce_fusion
  82.9 1.3 fusion.2
  85.0 1.2 copy.52
  86.2 4.5 %all-to-all-start = ((bf16[8,4,128,128]{3,2,1,0:T(8,128)(2,1)}), bf16[8,4,128,128]{3,2,1,0:T(8,128)(2,1)S(1)}, u32[]{:S(2)}, u32[]{:S(2)}) async-start(bf16[8,4,128,128]{3,2,1,0:T(8,128)(2,1)} %copy.52), calls=%async_computation | async-start | bytes 2097152 | tf_op jit(solution)/shard_map/all_to_all | solution.py:62
  92.6 22.3 %all-to-all-done = bf16[8,4,128,128]{3,2,1,0:T(8,128)(2,1)S(1)} async-done(((bf16[8,4,128,128]{3,2,1,0:T(8,128)(2,1)}), bf16[8,4,128,128]{3,2,1,0:T(8,128)(2,1)S(1)}, u32[]{:S(2)}, u32[]{:S(2)}) %all-to-all-start) | async-done | bytes 1048608 | tf_op jit(solution)/shard_map/all_to_all | solution.py:62
  114.9 2.2 gather_fusion.1
  117.1 1.8 broadcast_select_fusion.5
  120.4 28.8 %all_to_all.30 = bf16[8,4,128,128]{3,2,1,0:T(8,128)(2,1)S(1)} all-to-all(bf16[8,4,128,128]{3,2,1,0:T(8,128)(2,1)S(1)} %copy.54), channel_id=1, replica_groups=mesh['rows'=8,'shock'=4] {'rows'}, dimensions={0} | all-to-all | bytes 2097152 | tf_op jit(solution)/shard_map/all_to_all | solution.py:62
  149.2 2.2 gather_fusion.2
  151.4 1.8 broadcast_select_fusion.4
  154.7 28.8 %all_to_all.31 = bf16[8,4,128,128]{3,2,1,0:T(8,128)(2,1)S(1)} all-to-all(bf16[8,4,128,128]{3,2,1,0:T(8,128)(2,1)S(1)} %copy.56), channel_id=1, replica_groups=mesh['rows'=8,'shock'=4] {'rows'}, dimensions={0} | all-to-all | bytes 2097152 | tf_op jit(solution)/shard_map/all_to_all | solution.py:62
  183.5 2.2 gather_fusion.3
  185.7 1.8 broadcast_select_fusion.3
  189.0 28.7 %all_to_all.32 = bf16[8,4,128,128]{3,2,1,0:T(8,128)(2,1)S(1)} all-to-all(bf16[8,4,128,128]{3,2,1,0:T(8,128)(2,1)S(1)} %copy.58), channel_id=1, replica_groups=mesh['rows'=8,'shock'=4] {'rows'}, dimensions={0} | all-to-all | bytes 2097152 | tf_op jit(solution)/shard_map/all_to_all | solution.py:62
  217.7 2.2 gather_fusion.4
  219.8 1.8 broadcast_select_fusion.2
  223.2 28.7 %all_to_all.33 = bf16[8,4,128,128]{3,2,1,0:T(8,128)(2,1)S(1)} all-to-all(bf16[8,4,128,128]{3,2,1,0:T(8,128)(2,1)S(1)} %copy.60), channel_id=1, replica_groups=mesh['rows'=8,'shock'=4] {'rows'}, dimensions={0} | all-to-all | bytes 2097152 | tf_op jit(solution)/shard_map/all_to_all | solution.py:62
  251.9 2.2 gather_fusion.5
  254.0 1.8 broadcast_select_fusion.1
  257.8 1.2 copy.62
  259.0 3.6 %all-to-all-start.5 = ((bf16[8,4,128,128]{3,2,1,0:T(8,128)(2,1)}), bf16[8,4,128,128]{3,2,1,0:T(8,128)(2,1)S(1)}, u32[]{:S(2)}, u32[]{:S(2)}) async-start(bf16[8,4,128,128]{3,2,1,0:T(8,128)(2,1)} %copy.62), calls=%async_computation.5 | async-start | bytes 2097152 | tf_op jit(solution)/shard_map/all_to_all | solution.py:62
  262.6 1.7 copy.47
  264.2 23.8 %all-to-all-done.5 = bf16[8,4,128,128]{3,2,1,0:T(8,128)(2,1)S(1)} async-done(((bf16[8,4,128,128]{3,2,1,0:T(8,128)(2,1)}), bf16[8,4,128,128]{3,2,1,0:T(8,128)(2,1)S(1)}, u32[]{:S(2)}, u32[]{:S(2)}) %all-to-all-start.5) | async-done | bytes 1048608 | tf_op jit(solution)/shard_map/all_to_all | solution.py:62
  288.1 2.2 gather_fusion.6
  290.2 1.9 broadcast_select_fusion
  292.2 0.8 fusion.46
  293.0 5.7 %psum.23 = f32[4,128]{1,0:T(4,128)S(1)} all-reduce(f32[4,128]{1,0:T(4,128)S(1)} %get-tuple-element.8), channel_id=1, replica_groups=mesh['rows'=8,'shock'=4] {'shock'}, use_global_device_ids=true, to_apply=%region_8.10 | all-reduce | flops 512 | bytes 4096 | tf_op jit(solution)/shard_map/psum | solution.py:72
  298.7 0.8 multiply_divide_fusion
  (64 shorter events, 11.3 us)
Async XLA Ops:
  6.5 112.4 %copy-start = (bf16[4,16,128,128]{3,2,1,0:T(8,128)(2,1)S(1)}, bf16[4,16,128,128]{3,2,1,0:T(8,128)(2,1)}, u32[]{:S(2)}) copy-start(bf16[4,16,128,128]{3,2,1,0:T(8,128)(2,1)} %param.7) | copy-start | bytes 6291460
  6.5 75.4 %all-reduce.2.cloned.1.call-start = ((), (), s32[]{:S(2)}) async-start(), calls=%async_computation.6 | async-start | bytes 131072 | tf_op jit(solution)/shard_map/psum | solution.py:30
  84.3 1.9 copy-start.5
  85.0 5.8 %copy-start.7 = (s32[32,16]{0,1:T(8,128)S(1)}, s32[32,16]{0,1:T(8,128)}, u32[]{:S(2)}) copy-start(s32[32,16]{0,1:T(8,128)} %param.8) | copy-start | bytes 6148
  86.2 28.7 %all-to-all-start = ((bf16[8,4,128,128]{3,2,1,0:T(8,128)(2,1)}), bf16[8,4,128,128]{3,2,1,0:T(8,128)(2,1)S(1)}, u32[]{:S(2)}, u32[]{:S(2)}) async-start(bf16[8,4,128,128]{3,2,1,0:T(8,128)(2,1)} %copy.52), calls=%async_computation | async-start | bytes 2097152 | tf_op jit(solution)/shard_map/all_to_all | solution.py:62
  222.4 29.4 %copy-start.1 = (bf16[4,128,128]{2,1,0:T(8,128)(2,1)}, bf16[4,128,128]{2,1,0:T(8,128)(2,1)S(1)}, u32[]{:S(2)}) copy-start(bf16[4,128,128]{2,1,0:T(8,128)(2,1)S(1)} %fusion.14) | copy-start | bytes 393220
  256.6 0.7 copy-start.3
  259.0 29.0 %all-to-all-start.5 = ((bf16[8,4,128,128]{3,2,1,0:T(8,128)(2,1)}), bf16[8,4,128,128]{3,2,1,0:T(8,128)(2,1)S(1)}, u32[]{:S(2)}, u32[]{:S(2)}) async-start(bf16[8,4,128,128]{3,2,1,0:T(8,128)(2,1)} %copy.62), calls=%async_computation.5 | async-start | bytes 2097152 | tf_op jit(solution)/shard_map/all_to_all | solution.py:62
  290.2 1.9 copy-start.2
  290.2 1.9 copy-start.4
  290.2 1.9 copy-start.6
Sparse Core Ops, SparseCore 0:
  10.8 71.1 all-reduce.1
where the time goes:
time: 307 us; the launch traced here: 306 us
  blocking collectives  144 us (47%)
  waiting for transfers between devices  94.3 us (31%)
  local copies, waits for them, and re-layouts  21.2 us (7%)
  between operations  13.7 us (4%)
  other arithmetic  13.5 us (4%)
  matrix products  11.8 us (4%)
  starting transfers between devices  8.1 us (3%)
    all_to_all x4, blocking collectives, on_device(): lax.all_to_all(outgoing, 'rows', split_axis=0, concat_axis=0, tiled=True)  115 us
    psum x1, waiting for transfers between devices, on_device(): chosen, chosen_idio = lax.psum((chosen, chosen_idio), 'rows')  48.1 us
    all_to_all x2, waiting for transfers between devices, on_device(): lax.all_to_all(outgoing, 'rows', split_axis=0, concat_axis=0, tiled=True)  46.1 us
    psum x1, blocking collectives, on_device(): chosen, chosen_idio = lax.psum((chosen, chosen_idio), 'rows')  23.2 us
    gather x6, local copies, waits for them, and re-layouts, on_device(): jnp.take(stacked, take_index, axis=0)  13 us
    select_n x7, other arithmetic, on_device(): jnp.take(stacked, take_index, axis=0)  11.1 us
    all_to_all x2, starting transfers between devices, on_device(): lax.all_to_all(outgoing, 'rows', split_axis=0, concat_axis=0, tiled=True)  8.09 us
  transfers between devices with their start and end apart: 3, of which 3 were waited for; matrix products, arithmetic and copies ran while one was open for 2% of the time, Pallas kernels for 0%

commit v1 on v0

v1 whole, which is shorter than its diff:
```python
import functools

import jax
import jax.numpy as jnp
from jax import lax
from jax.experimental import pallas as pl
from jax.experimental.pallas import tpu as pltpu
from jax.sharding import PartitionSpec as P

HORIZONS = 7
CHUNKS = 2
HIGHEST = lax.Precision.HIGHEST
MESH = pl.DeviceIdType.MESH


def f32_dot(a, b, dims):
    return lax.dot_general(
        a, b, (dims, ((), ())), precision=HIGHEST, preferred_element_type=jnp.float32
    )


def kernel(
    owners,
    groups,
    capacity,
    relay,
    inv_ref,
    send_ref,
    coefs_ref,
    loadings_ref,
    idio_ref,
    shocked_ref,
    out_ref,
    dense,
    held,
    outgoing,
    parked,
    acc,
    squares,
    pick,
    part,
    parts,
    sums,
    row_sums,
    part_send,
    part_recv,
    sum_send,
    sum_recv,
    send_sem,
    recv_sem,
    fwd_send,
    fwd_recv,
    near_send,
    near_recv,
    tot_send,
    tot_recv,
):
    blk_dev, lags, size, _ = coefs_ref.shape
    local_rows = blk_dev * size
    shocks = shocked_ref.shape[1]
    factors = loadings_ref.shape[1]
    me = lax.axis_index("rows")
    col = lax.axis_index("shock")
    side = lax.rem(me, 2)
    twin = me + 1 - 2 * side
    lines = owners // 2
    line = me // 2

    def along(d):
        return lax.rem(line + d, lines) * 2 + side

    def copy(src, dst, send, recv, row, column):
        return pltpu.make_async_remote_copy(
            src_ref=src,
            dst_ref=dst,
            send_sem=send,
            recv_sem=recv,
            device_id=(row, column),
            device_id_type=MESH,
        )

    order = [d for pair in zip(range(1, lines), range(lines - 1, 0, -1)) for d in pair]
    order = list(dict.fromkeys(order))

    barrier = pltpu.get_barrier_semaphore()
    if relay:
        row_peers = [twin] + [along(d) for d in order]
        for v in row_peers:
            pl.semaphore_signal(barrier, inc=1, device_id=(v, col), device_id_type=MESH)
        n_peers = len(row_peers)
    else:

        def greet(d, _):
            v = lax.rem(me + d, owners)
            pl.semaphore_signal(barrier, inc=1, device_id=(v, col), device_id_type=MESH)
            return 0

        lax.fori_loop(1, owners, greet, 0)
        n_peers = owners - 1
    for d in range(1, groups):
        c = lax.rem(col + d, groups)
        pl.semaphore_signal(barrier, inc=1, device_id=(me, c), device_id_type=MESH)

    ids = lax.broadcasted_iota(jnp.int32, (local_rows, shocks), 0) + me * local_rows
    pick[...] = (ids == shocked_ref[...]).astype(jnp.float32)
    part[0:factors, :] = f32_dot(loadings_ref[...], pick[...], ((0,), (0,)))
    part[factors : factors + 8, :] = f32_dot(idio_ref[...], pick[...], ((1,), (0,)))
    pl.semaphore_wait(barrier, n_peers + groups - 1)

    if relay:
        first = copy(part, parts.at[0], part_send.at[0], part_recv.at[0], twin, col)
        first.start()
    else:

        def send_part(d, _):
            v = lax.rem(me + d, owners)
            copy(part, parts.at[d], part_send.at[d], part_recv.at[d], v, col).start()
            return 0

        lax.fori_loop(1, owners, send_part, 0)

    def place(o, _):
        for r in range(blk_dev):
            for q in range(capacity):
                at = inv_ref[r, o * capacity + q]
                block = coefs_ref[r, jnp.maximum(at, 0)]
                kept = jnp.where(at >= 0, block, jnp.zeros_like(block))
                dense[o, r * size : (r + 1) * size, q * size : (q + 1) * size] = kept
        return 0

    lax.fori_loop(0, owners, place, 0)

    if relay:
        first.wait()
        sums[...] = part[...] + parts[0]
        between = [
            copy(sums, parts.at[d], sum_send.at[d], sum_recv.at[d], along(d), col)
            for d in order
        ]
        for c in between:
            c.start()
        for c in between:
            c.wait()
        found = sums[...]
        for d in order:
            found = found + parts[d]
    else:

        def wait_part(d, _):
            v = lax.rem(me + d, owners)
            copy(part, parts.at[d], part_send.at[d], part_recv.at[d], v, col).wait()
            return 0

        lax.fori_loop(1, owners, wait_part, 0)
        sums[...] = part[...]

        def add_part(d, _):
            sums[...] += parts[d]
            return 0

        lax.fori_loop(1, owners, add_part, 0)
        found = sums[...]
    chosen = found[0:factors]
    chosen_idio = found[factors : factors + 1]
    scale = jnp.sqrt(jnp.sum(chosen * chosen, axis=0, keepdims=True) + chosen_idio)
    impact = f32_dot(loadings_ref[...], chosen, ((1,), (0,)))
    impact = (impact + pick[...] * chosen_idio) / scale
    start = impact.astype(jnp.bfloat16)
    squares[...] = start.astype(jnp.float32) ** 2
    mine = start.reshape(blk_dev, size, shocks)

    def add(p, owner):
        slab = held[p, owner].reshape(capacity * size, shocks)
        acc[...] += jnp.dot(dense[owner], slab, preferred_element_type=jnp.float32)

    rows_of = blk_dev // CHUNKS if relay else 0
    cuts = [pl.ds(c * rows_of, rows_of) for c in range(CHUNKS)] if relay else []

    def relay_step(p):
        sends = []
        for c, cut in enumerate(cuts):
            here = held.at[p, me, cut]
            for d in order:
                k = d * CHUNKS + c
                one = copy(here, here, send_sem.at[k], recv_sem.at[p, k], along(d), col)
                one.start()
                sends.append(one)
            one = copy(here, here, near_send.at[c], near_recv.at[p, c], twin, col)
            one.start()
            sends.append(one)
        acc[...] = jnp.zeros_like(acc)
        add(p, me)
        for d in order:
            src = along(lines - d)
            for c, cut in enumerate(cuts):
                k = d * CHUNKS + c
                there = held.at[p, src, cut]
                copy(there, there, send_sem.at[k], recv_sem.at[p, k], src, col).wait_recv()
                one = copy(there, there, fwd_send.at[k], fwd_recv.at[p, k], twin, col)
                one.start()
                sends.append(one)
            add(p, src)
        for c, cut in enumerate(cuts):
            there = held.at[p, twin, cut]
            copy(there, there, near_send.at[c], near_recv.at[p, c], twin, col).wait_recv()
        add(p, twin)
        for d in order:
            src = lax.rem(line + lines - d, lines) * 2 + 1 - side
            for c, cut in enumerate(cuts):
                k = d * CHUNKS + c
                there = held.at[p, src, cut]
                copy(there, there, fwd_send.at[k], fwd_recv.at[p, k], twin, col).wait_recv()
            add(p, src)
        for one in sends:
            one.wait_send()

    def direct_copy(p, d):
        v = lax.rem(me + d, owners)
        return copy(
            outgoing.at[v], held.at[p, me], send_sem.at[d], recv_sem.at[p, d], v, col
        )

    def direct_step(p):
        def go(d, _):
            direct_copy(p, d).start()
            return 0

        lax.fori_loop(1, owners, go, 0)
        acc[...] = jnp.zeros_like(acc)
        held[p, me] = outgoing[me]
        add(p, me)

        def take(d, _):
            src = lax.rem(me + owners - d, owners)
            there = held.at[p, src]
            copy(there, there, send_sem.at[d], recv_sem.at[p, d], src, col).wait_recv()
            add(p, src)
            return 0

        lax.fori_loop(1, owners, take, 0)

        def sent(d, _):
            direct_copy(p, d).wait_send()
            return 0

        lax.fori_loop(1, owners, sent, 0)

    def stage(p, blocks):
        if relay:
            held[p, me] = blocks
        else:
            parked[...] = blocks

            def fill(v, _):
                for w in range(capacity):
                    outgoing[v, w] = parked[send_ref[v, w]]
                return 0

            lax.fori_loop(0, owners, fill, 0)

    stage(0, mine)

    def horizon(h, _):
        p = lax.rem(h, 2)
        (relay_step if relay else direct_step)(p)
        now = acc[...].astype(jnp.bfloat16)
        squares[...] += now.astype(jnp.float32) ** 2
        stage(1 - p, now.reshape(blk_dev, size, shocks))
        return 0

    lax.fori_loop(0, HORIZONS - 1, horizon, 0)

    ones = jnp.ones((8, shocks), jnp.float32)
    row_sums[0] = f32_dot(ones, squares[...], ((1,), (1,)))
    tots = []
    for d in range(1, groups):
        c = lax.rem(col + d, groups)
        one = copy(row_sums.at[0], row_sums.at[d], tot_send.at[d], tot_recv.at[d], me, c)
        one.start()
        tots.append(one)
    for one in tots:
        one.wait()
    total = row_sums[0]
    for d in range(1, groups):
        total = total + row_sums[d]
    first_row = (lax.broadcasted_iota(jnp.int32, (8, shocks), 0) == 0).astype(jnp.float32)
    spread = f32_dot(total, first_row, ((0,), (0,)))
    out_ref[...] = (shocks * groups) * squares[...] / (spread + 1e-06)


def on_device(coefs, lag_pattern, loadings, idiosyncratic, shocked):
    blk_dev, lags, size, _ = coefs.shape
    owners = lax.axis_size("rows")
    groups = lax.axis_size("shock")
    mine = lax.axis_index("rows")
    capacity = min(blk_dev, max(1, blk_dev * lags // owners))
    relay = capacity == blk_dev and owners % 2 == 0 and blk_dev % CHUNKS == 0
    shocks = shocked.shape[0]
    local_rows = blk_dev * size
    factors = loadings.shape[1]
    n_blocks = owners * blk_dev
    my_lags = lax.dynamic_slice_in_dim(lag_pattern, mine * blk_dev, blk_dev, 0)
    if capacity == blk_dev:
        take = my_lags
        send = jnp.broadcast_to(jnp.arange(blk_dev, dtype=jnp.int32), (owners, blk_dev))
    else:
        ids = jnp.arange(n_blocks, dtype=jnp.int32)
        read = jnp.any(my_lags.reshape(-1, 1) == ids[None, :], axis=0)
        earlier = (ids[:, None] > ids[None, :]) & (
            ids[:, None] // blk_dev == ids[None, :] // blk_dev
        )
        before = jnp.sum(earlier & read[None, :], axis=1, dtype=jnp.int32)
        slot = ids // blk_dev * capacity + before
        hit = my_lags[:, :, None] == ids[None, None, :]
        take = jnp.sum(jnp.where(hit, slot[None, None, :], 0), axis=2)
        reads = lag_pattern.reshape(owners, blk_dev * lags)
        own = mine * blk_dev + jnp.arange(blk_dev, dtype=jnp.int32)
        need = jnp.any(reads[:, :, None] == own[None, None, :], axis=1)
        q = jnp.arange(blk_dev, dtype=jnp.int32)
        ahead = jnp.sum(
            (q[:, None] > q[None, :])[None] & need[:, None, :], axis=2, dtype=jnp.int32
        )
        w = jnp.arange(capacity, dtype=jnp.int32)
        routed = need[:, None, :] & (ahead[:, None, :] == w[None, :, None])
        send = jnp.sum(jnp.where(routed, q[None, None, :], 0), axis=2)
    slots = jnp.arange(owners * capacity, dtype=jnp.int32)
    at = take[:, :, None] == slots[None, None, :]
    lag_ids = jnp.arange(lags, dtype=jnp.int32)[None, :, None]
    inv = jnp.max(jnp.where(at, lag_ids, -1), axis=1)
    idio = jnp.broadcast_to(idiosyncratic[None, :], (8, local_rows))

    vmem = pl.BlockSpec(memory_space=pltpu.VMEM)
    smem = pl.BlockSpec(memory_space=pltpu.SMEM)
    n_sem = owners * CHUNKS
    tall = factors + 8
    dma = pltpu.SemaphoreType.DMA
    n_out = 1 if relay else owners
    return pl.pallas_call(
        functools.partial(kernel, owners, groups, capacity, relay),
        out_shape=jax.ShapeDtypeStruct((local_rows, shocks), jnp.float32),
        in_specs=[smem, smem, vmem, vmem, vmem, vmem],
        out_specs=vmem,
        scratch_shapes=[
            pltpu.VMEM((owners, local_rows, capacity * size), jnp.bfloat16),
            pltpu.VMEM((2, owners, capacity, size, shocks), jnp.bfloat16),
            pltpu.VMEM((n_out, capacity, size, shocks), jnp.bfloat16),
            pltpu.VMEM((blk_dev, size, shocks), jnp.bfloat16),
            pltpu.VMEM((local_rows, shocks), jnp.float32),
            pltpu.VMEM((local_rows, shocks), jnp.float32),
            pltpu.VMEM((local_rows, shocks), jnp.float32),
            pltpu.VMEM((tall, shocks), jnp.float32),
            pltpu.VMEM((owners, tall, shocks), jnp.float32),
            pltpu.VMEM((tall, shocks), jnp.float32),
            pltpu.VMEM((groups, 8, local_rows), jnp.float32),
            dma((owners,)),
            dma((owners,)),
            dma((owners,)),
            dma((owners,)),
            dma((n_sem,)),
            dma((2, n_sem)),
            dma((n_sem,)),
            dma((2, n_sem)),
            dma((CHUNKS,)),
            dma((2, CHUNKS)),
            dma((groups,)),
            dma((groups,)),
        ],
        compiler_params=pltpu.CompilerParams(
            collective_id=0, has_side_effects=True, vmem_limit_bytes=40 * 2**20
        ),
    )(inv, send.astype(jnp.int32), coefs, loadings, idio, shocked[None, :])


def solution(mesh):
    placed = (P("rows", None, None, None), P(), P("rows", None), P("rows"), P("shock"))
    return jax.shard_map(
        on_device, mesh=mesh, in_specs=placed, out_specs=P("rows", "shock"), check_vma=False
    )
```

time: 307 us -> 121 us (0.39)
  blocking collectives: 144 us -> 0 us
  Pallas kernels: 0 us -> 114 us
  waiting for transfers between devices: 94.3 us -> 0 us
  local copies, waits for them, and re-layouts: 21.2 us -> 5.44 us
  between operations: 13.7 us -> 0.02 us
  other arithmetic: 13.5 us -> 0.09 us
  matrix products: 11.8 us -> 0 us
  starting transfers between devices: 8.1 us -> 0 us
    all_to_all x4 -> x0, blocking collectives: 115 us -> none  [on_device(): lax.all_to_all(outgoing, 'rows', split_axis=0, concat_axis=0, tiled=True)]
    pallas_call x0 -> x1, Pallas kernels: none -> 114 us  [on_device(): pl.pallas_call(functools.partial(kernel, owners, groups, capacity, relay)...]
    psum x1 -> x0, waiting for transfers between devices: 48.1 us -> none  [on_device(): chosen, chosen_idio = lax.psum((chosen, chosen_idio), 'rows')]
    all_to_all x2 -> x0, waiting for transfers between devices: 46.1 us -> none  [on_device(): lax.all_to_all(outgoing, 'rows', split_axis=0, concat_axis=0, tiled=True)]
    psum x2 -> x0, blocking collectives: 28.9 us -> none  [the longest x1 23.2 us: on_device(): chosen, chosen_idio = lax.psum((chosen, chosen_idio), 'rows')]
    gather x7 -> x0, local copies, waits for them, and re-layouts: 13.8 us -> none  [the longest x6 13 us: on_device(): jnp.take(stacked, take_index, axis=0)]
    dot_general x15 -> x0, matrix products: 11.8 us -> none  [the longest x6 4.53 us: on_device(): jnp.einsum('rlij,rljs->ris', coefs, lagged, preferred_element_type=jnp.fl...]
    select_n x8 -> x0, other arithmetic: 11.1 us -> none  [the longest x7 11.1 us: on_device(): jnp.take(stacked, take_index, axis=0)]
  transfers between devices with their start and end apart: 3 -> 0, of which waited for: 3 -> 0; matrix products, arithmetic and copies ran while one was open for 2% -> 0% of each run, Pallas kernels for 0% -> 0%
where the time goes in v1:
time: 121 us; the launch traced here: 120 us
  Pallas kernels  114 us (94%)
  local copies, waits for them, and re-layouts  5.44 us (4%)
    pallas_call x1, Pallas kernels, on_device(): pl.pallas_call(functools.partial(kernel, owners, groups, capacity, relay)...  114 us
    unnamed x9, local copies, waits for them, and re-layouts  4.59 us

profile of v1, /device:TPU:0, one launch (start us, length us, event | category | flops | bytes accessed | tf_op | source)
XLA Modules:
  0.0 119.8 jit_solution(10710589143508906516)
XLA Ops:
  0.0 0.0 copy-start
  0.0 0.7 copy-done
  0.7 0.1 constant_dynamic-slice_fusion
  0.8 0.1 copy.7
  0.9 0.1 select_reduce_fusion.inv_ref
  1.0 0.7 broadcast_in_dim.30.idio_ref
  1.6 0.0 copy-start.1
  1.6 1.6 %copy-done.1 = bf16[4,16,128,128]{3,2,1,0:T(8,128)(2,1)S(1)} copy-done((bf16[4,16,128,128]{3,2,1,0:T(8,128)(2,1)S(1)}, bf16[4,16,128,128]{3,2,1,0:T(8,128)(2,1)}, u32[]{:S(2)}) %copy-start.1) | copy-done | bytes 2097176
  3.2 0.0 copy-start.2
  3.2 0.9 copy-done.2
  4.2 0.0 copy-start.3
  4.2 0.7 copy-done.3
  4.8 114.2 %shard_map.55 = f32[512,128]{1,0:T(8,128)S(1)} custom-call(s32[4,32]{1,0:T(4,128)S(1)} %select_reduce_fusion.inv_ref, s32[8,4]{1,0:T(8,128)S(1)} %broadcast_in_dim.29.send_ref, bf16[4,16,128,128]{3,2,1,0:T(8,128)(2,1)S(1)} %copy-done.1, f32[512,128]{1,0:T(8,128)S(1)} %copy-done.2, f32[8,512]{1,0:T(8,128)S(1)} %broadcast_in_dim.30.idio_ref, s32[1,128]{1,0:T(1,128)S(1)} %bitcast.1), custom_call_target="tpu_custom_call" | custom-call | tf_op jit(solution)/shard_map/pallas_call | solution.py:338
  119.1 0.7 copy.9
  (1 shorter events, 0.0 us)
Async XLA Ops:
  0.0 0.7 copy-start
  1.6 1.6 %copy-start.1 = (bf16[4,16,128,128]{3,2,1,0:T(8,128)(2,1)S(1)}, bf16[4,16,128,128]{3,2,1,0:T(8,128)(2,1)}, u32[]{:S(2)}) copy-start(bf16[4,16,128,128]{3,2,1,0:T(8,128)(2,1)} %coefs_ref.1) | copy-start | bytes 6291460
  3.2 0.9 copy-start.2
  4.2 0.7 copy-start.3
